TPU v7x, 32 devices: a whole 2x2x4 slice. The times are simulated.
32 devices in a mesh: outer: 4 (over y, x), inner: 8 (over z, core).
Axes of the slice: x: 2, y: 2, z: 4, core: 2. Of those that a mesh axis runs over, the one named last changes fastest.
Arguments:
- queries: bfloat16 [49152, 2048], P(('outer', 'inner')), may hold values from -6 to 6
- keys: bfloat16 [49152, 2048], P(('outer', 'inner')), may hold values from -6 to 6
- values: bfloat16 [49152, 2048], P(('outer', 'inner')), may hold values from -6 to 6
- gain: float32 [2048], replicated, may hold values from 0.5 to 1.5
- tile_doc: int32 [384], P(('outer', 'inner')), may hold values from 0 to 7, as said below
- tile_fill: int32 [384], P(('outer', 'inner')), may hold values from 1 to 128, as said below
Outputs:
- attended: bfloat16 [49152, 2048], P(('outer', 'inner'))
Inputs may be any that keep to these rules, and one draw needn't show every extreme that they name: tile_doc is 0 at the first tile and rises by 0 or 1 from each tile to the next, so each document holds whole consecutive tiles; the window holds exactly 8 documents. tile_fill is 128 on every tile except the last tile of each document.
All inputs are finite; a program needn't handle non-finite values.
Results may differ from a plain program's by a relative error of at most 0.0027.
Values sent between devices are 32-bit elements; how exact they have to be, the bound alone decides.
A program may use at most 192 MiB of HBM per device.

v0:
```python
from functools import reduce

import jax
import jax.numpy as jnp
from jax import lax
from jax.sharding import PartitionSpec as P

HEADS = 16
HEAD = 128
TILE = 128
BLOCK = 512


def shifted(value, axis, by):
    length = lax.axis_size(axis)
    pairs = [(i, i + by) for i in range(length) if 0 <= i + by < length]
    return lax.ppermute(value, axis, pairs)


def entering(value, axis, join, neutral):
    count, mine = (lax.axis_size(axis), lax.axis_index(axis))
    pieces = jax.tree.map(lambda part: lax.all_gather(part, axis), value)
    so_far = jax.tree.map(
        lambda part, zero: jnp.full_like(part, 0) + jnp.asarray(zero, part.dtype), value, neutral
    )

    def lap(position, so_far):
        longer = join(so_far, jax.tree.map(lambda part: part[position], pieces))
        return jax.tree.map(lambda new, old: jnp.where(position < mine, new, old), longer, so_far)

    return lax.fori_loop(0, count - 1, lap, so_far)


def spread(value, axis, source):
    kept = jnp.where(lax.axis_index(axis) == source, value, 0).astype(value.dtype)
    return lax.psum(kept, axis)


def combine(first, second):
    first_state, first_last, first_single = first
    second_state, second_last, second_single = second
    second_none = second_last[0] == 0
    first_none = first_last[0] == 0
    keep = jnp.logical_or(
        second_none, jnp.logical_and(second_single[0] == 1, second_last[0] == first_last[0])
    )
    state = jnp.where(keep, second_state + first_state, second_state)
    last = jnp.where(second_none, first_last, second_last)
    same = (first_last == second_last).astype(jnp.int32)
    single = jnp.where(
        second_none,
        first_single,
        jnp.where(first_none, second_single, first_single * second_single * same),
    )
    return (state, last, single)


def summarize(key_rows, value_rows, docs, real):
    last_doc = docs[-1]
    chosen = jnp.logical_and(docs == last_doc, real)
    masked = jnp.where(chosen[:, None, None], key_rows, jnp.zeros_like(key_rows))
    state = jnp.einsum("thd,the->hde", masked, value_rows, preferred_element_type=jnp.float32)
    last = (last_doc + 1).reshape(1)
    single = (docs[0] == last_doc).astype(jnp.int32).reshape(1)
    return (state, last, single)


def direct_part(query_rows, key_rows, value_rows, docs, real):
    length = query_rows.shape[0]
    scores = jnp.einsum("qhd,khd->hqk", query_rows, key_rows, preferred_element_type=jnp.float32)
    places = jnp.arange(length)
    allowed = (
        (places[:, None] >= places[None, :]) & (docs[:, None] == docs[None, :]) & real[None, :]
    )
    weights = jnp.where(allowed[None], scores, 0.0).astype(jnp.bfloat16)
    return jnp.einsum("hqk,khd->qhd", weights, value_rows, preferred_element_type=jnp.float32)


def finish(direct, query_rows, docs, real, carry, gain):
    state, last, single = carry
    carried = jnp.einsum(
        "qhd,hde->qhe", query_rows.astype(jnp.float32), state, precision=lax.Precision.HIGHEST
    )
    uses = docs + 1 == last[0]
    raw = direct + jnp.where(uses[:, None, None], carried, 0.0)
    raw = jnp.where(real[:, None, None], raw, 0.0)
    meansq = jnp.mean(raw * raw, axis=-1, keepdims=True)
    normed = raw * lax.rsqrt(meansq + 1e-06) * gain.reshape(HEADS, HEAD)
    return normed.astype(jnp.bfloat16).reshape(query_rows.shape[0], HEADS * HEAD)


def empty_state():
    return (
        jnp.zeros((HEADS, HEAD, HEAD), jnp.float32),
        jnp.zeros((1,), jnp.int32),
        jnp.zeros((1,), jnp.int32),
    )


def across_groups(total):
    earlier = empty_state()
    for step in range(lax.axis_size("outer") - 1):
        running = combine(earlier, total)
        earlier = shifted((running[0], running[1], running[2]), "outer", 1)
    return earlier


def body(queries, keys, values, gain, tile_doc, tile_fill):
    length = queries.shape[0]
    count = length // BLOCK
    docs = jnp.repeat(tile_doc, TILE)
    real = jnp.arange(length, dtype=jnp.int32) % TILE < jnp.repeat(tile_fill, TILE)
    query_all = queries.reshape(length, HEADS, HEAD)
    key_all = keys.reshape(length, HEADS, HEAD)
    value_all = values.reshape(length, HEADS, HEAD)
    directs = []
    summaries = []
    for block in range(count):
        lower = block * BLOCK
        upper = lower + BLOCK
        directs.append(
            direct_part(
                query_all[lower:upper],
                key_all[lower:upper],
                value_all[lower:upper],
                docs[lower:upper],
                real[lower:upper],
            )
        )
        summaries.append(
            summarize(
                key_all[lower:upper], value_all[lower:upper], docs[lower:upper], real[lower:upper]
            )
        )
    own = reduce(combine, summaries)
    before_inner = entering(own, "inner", combine, empty_state())
    through = combine(before_inner, own)
    total = (
        spread(through[0], "inner", lax.axis_size("inner") - 1),
        spread(through[1], "inner", lax.axis_size("inner") - 1),
        spread(through[2], "inner", lax.axis_size("inner") - 1),
    )
    prefix = combine(across_groups(total), before_inner)
    carry = prefix
    results = []
    for block in range(count):
        lower = block * BLOCK
        upper = lower + BLOCK
        results.append(
            finish(
                directs[block],
                query_all[lower:upper],
                docs[lower:upper],
                real[lower:upper],
                carry,
                gain,
            )
        )
        carry = combine(carry, summaries[block])
    return jnp.concatenate(results, axis=0)


def solution(mesh):
    placed = (
        P(("outer", "inner"), None),
        P(("outer", "inner"), None),
        P(("outer", "inner"), None),
        P(),
        P(("outer", "inner")),
        P(("outer", "inner")),
    )
    return jax.shard_map(
        body, mesh=mesh, in_specs=placed, out_specs=P(("outer", "inner"), None), check_vma=False
    )
```

profile of v0, /device:TPU:0, one launch (start us, length us, event | category | flops | bytes accessed | tf_op | source)
XLA Modules:
  0.0 397.2 jit_solution(3273020750897445659)
XLA Ops:
  14.4 1.8 fusion.54
  16.3 5.9 %fusion.52 = (bf16[512,2048]{1,0:T(8,128)(2,1)}, bf16[512,2048]{1,0:T(8,128)(2,1)S(1)}, bf16[512,2048]{1,0:T(8,128)(2,1)}) fusion(bf16[1536,2048]{1,0:T(8,128)(2,1)} %param.9), kind=kLoop, calls=%fused_computation.91 | loop fusion | bytes 12582912 | tf_op jit(solution)/shard_map/slice | solution.py:124
  22.1 3.9 copy.108
  26.1 5.8 %fusion.53 = (bf16[512,2048]{1,0:T(8,128)(2,1)}, bf16[512,2048]{1,0:T(8,128)(2,1)}, bf16[512,2048]{1,0:T(8,128)(2,1)}) fusion(bf16[1536,2048]{1,0:T(8,128)(2,1)} %param.10), kind=kLoop, calls=%fused_computation.92 | loop fusion | bytes 12582912 | tf_op jit(solution)/shard_map/slice | solution.py:125
  31.9 4.0 copy.69
  35.8 3.9 copy.111
  39.8 3.9 copy.112
  43.7 2.5 copy.109
  46.2 4.1 %copy.110 = bf16[512,2048]{0,1:T(8,128)(2,1)} copy(bf16[512,2048]{1,0:T(8,128)(2,1)} %get-tuple-element.205) | data formatting | bytes 4194304
  50.2 2.4 fusion.7
  55.7 1.7 add_select_fusion.7
  60.0 1.3 dynamic-update-slice.1
  62.0 10.7 %all-reduce.3 = (s32[8]{0:T(128)S(1)}, s32[8]{0:T(128)S(1)}) all-reduce(s32[8]{0:T(128)S(1)} %dynamic-update-slice, s32[8]{0:T(128)S(1)} %dynamic-update-slice.1), channel_id=2, replica_groups=mesh['outer'=4,'inner'=8] {'inner'}, use_global_device_ids=true, to_apply=%add | all-reduce | flops 16 | bytes 128
  72.8 69.7 %all-gather.5.cloned.1.call-done = f32[128,128,128]{2,1,0:T(8,128)} async-done(((f32[16,128,128]{2,1,0:T(8,128)}), f32[128,128,128]{2,1,0:T(8,128)}) %all-gather.5.cloned.1.call-update) | async-done | bytes 8388624 | tf_op jit(solution)/shard_map/all_gather | solution.py:22
  142.4 54.9 %while.18 = (s32[]{:T(128)}, f32[16,128,128]{2,1,0:T(8,128)S(1)}, s32[1]{0:T(128)}, s32[1]{0:T(128)}, s32[]{:T(128)}, /*index=5*/s32[8,1]{0,1:T(1,128)S(1)}, s32...) while((s32[]{:T(128)}, f32[16,128,128]{2,1,0:T(8,128)S(1)}, ...), condition=%wide.region_1.2_spmd.clone, body=%wide.region_0.1_spmd.clone.sunk | while | flops 1048594 | bytes 3146019 | solution.py:31
  147.8 1.7 fusion.79
  155.7 1.7 fusion.79
  163.5 1.7 fusion.79
  171.4 1.7 fusion.79
  179.2 1.7 fusion.79
  187.1 1.7 fusion.79
  194.9 1.7 fusion.79
  199.1 57.4 %all-reduce.6.cloned.1.call-done = f32[16,128,128]{2,1,0:T(8,128)} async-done(((f32[16,128,128]{2,1,0:T(8,128)}), f32[16,128,128]{2,1,0:T(8,128)}) %all-reduce.6.cloned.1.call-update) | async-done | bytes 1048592 | tf_op jit(solution)/shard_map/psum | solution.py:36
  256.6 4.3 %collective-permute-start.3 = (f32[16,128,128]{2,1,0:T(8,128)}, f32[16,128,128]{2,1,0:T(8,128)}, u32[]{:S(2)}, u32[]{:S(2)}) collective-permute-start(f32[16,128,128]{2,1,0:T(8,128)} %all-reduce.6.cloned.1.call-done), channel_id=1, source_target_pairs={{0,8},{8,16},{16,24},{1,9},{9,17},{17,25},{2,10},{10,18},{18,26},{... | collective-permute-start | bytes 3145736 | tf_op jit(solution)/shard_map/ppermute | solution.py:17
  262.0 5.7 %fusion.51 = (bf16[512,2048]{1,0:T(8,128)(2,1)}, bf16[512,2048]{1,0:T(8,128)(2,1)}, bf16[512,2048]{1,0:T(8,128)(2,1)}) fusion(bf16[1536,2048]{1,0:T(8,128)(2,1)} %param.8), kind=kLoop, calls=%fused_computation.90 | loop fusion | bytes 12582912 | tf_op jit(solution)/shard_map/slice | solution.py:123
  268.9 2.9 copy.114
  271.8 7.8 %all-reduce.2 = (s32[1]{0:T(128)}, s32[1]{0:T(128)}) all-reduce(s32[1]{0:T(128)S(6)} %select_n.305, s32[1]{0:T(128)S(6)} %select_n.313), channel_id=1, replica_groups=mesh['outer'=4,'inner'=8] {'inner'}, use_global_device_ids=true, to_apply=%region_2.3 | all-reduce | flops 2 | bytes 16 | tf_op jit(solution)/shard_map/psum | solution.py:36
  280.8 3.7 collective-permute-start
  286.4 2.8 add_select_fusion.5
  289.1 4.5 %collective-permute-start.4 = (f32[16,128,128]{2,1,0:T(8,128)}, f32[16,128,128]{2,1,0:T(8,128)}, u32[]{:S(2)}, u32[]{:S(2)}) collective-permute-start(f32[16,128,128]{2,1,0:T(8,128)} %add_select_fusion.5), channel_id=1, source_target_pairs={{0,8},{8,16},{16,24},{1,9},{9,17},{17,25},{2,10},{10,18},{18,26},{... | collective-permute-start | bytes 3145736 | tf_op jit(solution)/shard_map/ppermute | solution.py:17
  293.6 9.4 %fusion.6 = f32[16,512,128]{1,2,0:T(8,128)} fusion(bf16[512,16,128]{0,2,1:T(8,128)(2,1)} %bitcast.158, bf16[512,16,128]{0,2,1:T(8,128)(2,1)S(1)} %bitcast.138, bf16[512,16,128]{0,2,1:T(8,128)(2,1)} %bitcast.156, pred[512,512]{1,0:T(8,128)(4,1)} %get-tuple-element.236), kind=kOutput, calls=%fused_computation.22 | convolution fusion | flops 2155872256 | bytes 10747904 | tf_op jit(solution)/shard_map/hqk,khd->qhd/dot_general | solution.py:76
  303.0 3.9 copy.113
  306.9 3.9 copy.107
  311.8 10.0 %fusion.5 = f32[16,512,128]{1,2,0:T(8,128)} fusion(bf16[512,16,128]{0,2,1:T(8,128)(2,1)} %bitcast.154, bf16[512,16,128]{0,2,1:T(8,128)(2,1)} %bitcast.142, bf16[512,16,128]{0,2,1:T(8,128)(2,1)} %bitcast.152, pred[512,512]{1,0:T(8,128)(4,1)S(1)} %get-tuple-element.235), kind=kOutput, calls=%fused_computation.21 | convolution fusion | flops 2155872256 | bytes 10747904 | tf_op jit(solution)/shard_map/hqk,khd->qhd/dot_general | solution.py:76
  323.0 4.7 %collective-permute-start.1 = (s32[1]{0:T(128)}, s32[1]{0:T(128)}, u32[]{:S(2)}, u32[]{:S(2)}) collective-permute-start(s32[1]{0:T(128)} %select_n.307), channel_id=1, source_target_pairs={{0,8},{8,16},{16,24},{1,9},{9,17},{17,25},{2,10},{10,18},{18,26},{... | collective-permute-start | bytes 20 | tf_op jit(solution)/shard_map/ppermute | solution.py:17
  329.0 2.6 add_select_fusion.4
  331.7 5.1 %collective-permute-start.5 = (f32[16,128,128]{2,1,0:T(8,128)}, f32[16,128,128]{2,1,0:T(8,128)}, u32[]{:S(2)}, u32[]{:S(2)}) collective-permute-start(f32[16,128,128]{2,1,0:T(8,128)} %add_select_fusion.4), channel_id=1, source_target_pairs={{0,8},{8,16},{16,24},{1,9},{9,17},{17,25},{2,10},{10,18},{18,26},{... | collective-permute-start | bytes 3145736 | tf_op jit(solution)/shard_map/ppermute | solution.py:17
  336.8 10.0 %fusion.4 = f32[16,512,128]{1,2,0:T(8,128)} fusion(bf16[512,16,128]{0,2,1:T(8,128)(2,1)} %bitcast.151, bf16[512,16,128]{0,2,1:T(8,128)(2,1)} %bitcast.140, bf16[512,16,128]{0,2,1:T(8,128)(2,1)} %bitcast.148, pred[512,512]{1,0:T(8,128)(4,1)S(1)} %copy-done.13), kind=kOutput, calls=%fused_computation.20 | convolution fusion | flops 2155872256 | bytes 10747904 | tf_op jit(solution)/shard_map/hqk,khd->qhd/dot_general | solution.py:76
  348.0 7.1 %collective-permute-start.2 = (s32[1]{0:T(128)}, s32[1]{0:T(128)}, u32[]{:S(2)}, u32[]{:S(2)}) collective-permute-start(s32[1]{0:T(128)} %select_n.308), channel_id=1, source_target_pairs={{0,8},{8,16},{16,24},{1,9},{9,17},{17,25},{2,10},{10,18},{18,26},{... | collective-permute-start | bytes 20 | tf_op jit(solution)/shard_map/ppermute | solution.py:17
  356.7 1.9 add_select_fusion.2
  359.5 4.1 %multiply_reduce_fusion = (f32[512,16]{0,1:T(8,128)S(1)}, f32[512,16,128]{0,2,1:T(8,128)S(1)}) fusion(bf16[512,16,128]{0,2,1:T(8,128)(2,1)S(1)} %bitcast.139, f32[16,128,128]{2,1,0:T(8,128)} %copy-done.11, f32[16,128,128]{2,1,0:T(8,128)S(1)} %add_select_fusion.2, pred[]{:T(512)S(6)} %or.55, pred[512]{0:T(512)(128)(4,1)S(1)} %get-tuple-element.234, ...), kind=kOutput, calls=%fused_computation.15 | convolution fusion | flops 1616371712 | bytes 12616705 | tf_op jit(solution)/shard_map/qhd,hde->qhe/dot_general | solution.py:81
  363.7 2.6 multiply_reduce_fusion.1
  366.6 4.0 multiply_reduce_fusion.2
  370.6 3.6 multiply_convert_fusion.2
  374.1 2.9 copy.89
  377.0 4.0 copy.90
  381.0 4.0 copy.91
  385.0 5.4 %pad_maximum_fusion = bf16[1536,2048]{1,0:T(8,128)(2,1)} fusion(bf16[512,2048]{1,0:T(8,128)(2,1)} %copy.91, bf16[512,2048]{1,0:T(8,128)(2,1)} %copy.90, bf16[512,2048]{1,0:T(8,128)(2,1)S(1)} %copy.89), kind=kLoop, calls=%fused_computation.7 | loop fusion | flops 18874368 | bytes 12582912 | tf_op jit(solution)/shard_map/concatenate | solution.py:160
  (79 shorter events, 22.4 us)
Async XLA Ops:
  6.5 135.9 %all-gather.5.cloned.1.call-start = ((), (), s32[]{:S(2)}) async-start(), calls=%async_computation.1 | async-start | bytes 9437184 | tf_op jit(solution)/shard_map/all_gather | solution.py:22
  46.2 4.1 %copy-start.6 = (bf16[512,2048]{0,1:T(8,128)(2,1)S(1)}, bf16[512,2048]{0,1:T(8,128)(2,1)}, u32[]{:S(2)}) copy-start(bf16[512,2048]{0,1:T(8,128)(2,1)} %copy.108) | copy-start | bytes 6291460
  50.2 2.5 copy-start.7
  50.2 2.9 copy-start.8
  52.7 1.1 copy-start.12
  53.1 1.6 copy-start.9
  53.1 2.6 copy-start.10
  53.8 3.6 copy-start.11
  55.7 3.1 copy-start.15
  57.5 199.1 %all-reduce.6.cloned.1.call-start = ((), (), s32[]{:S(2)}) async-start(), calls=%async_computation | async-start | bytes 2097152 | tf_op jit(solution)/shard_map/psum | solution.py:36
  142.4 55.5 %copy-start.5 = (f32[16,128,128]{2,1,0:T(8,128)S(1)}, f32[16,128,128]{2,1,0:T(8,128)}, u32[]{:S(2)}) copy-start(f32[16,128,128]{2,1,0:T(8,128)} %add_select_fusion.7) | copy-start | bytes 3145732
  256.6 29.8 %collective-permute-start.3 = (f32[16,128,128]{2,1,0:T(8,128)}, f32[16,128,128]{2,1,0:T(8,128)}, u32[]{:S(2)}, u32[]{:S(2)}) collective-permute-start(f32[16,128,128]{2,1,0:T(8,128)} %all-reduce.6.cloned.1.call-done), channel_id=1, source_target_pairs={{0,8},{8,16},{16,24},{1,9},{9,17},{17,25},{2,10},{10,18},{18,26},{... | collective-permute-start | bytes 3145736 | tf_op jit(solution)/shard_map/ppermute | solution.py:17
  280.8 4.3 %collective-permute-start = (s32[1]{0:T(128)}, s32[1]{0:T(128)}, u32[]{:S(2)}, u32[]{:S(2)}) collective-permute-start(s32[1]{0:T(128)} %select_n.306), channel_id=1, source_target_pairs={{0,8},{8,16},{16,24},{1,9},{9,17},{17,25},{2,10},{10,18},{18,26},{... | collective-permute-start | bytes 20 | tf_op jit(solution)/shard_map/ppermute | solution.py:17
  289.1 39.9 %collective-permute-start.4 = (f32[16,128,128]{2,1,0:T(8,128)}, f32[16,128,128]{2,1,0:T(8,128)}, u32[]{:S(2)}, u32[]{:S(2)}) collective-permute-start(f32[16,128,128]{2,1,0:T(8,128)} %add_select_fusion.5), channel_id=1, source_target_pairs={{0,8},{8,16},{16,24},{1,9},{9,17},{17,25},{2,10},{10,18},{18,26},{... | collective-permute-start | bytes 3145736 | tf_op jit(solution)/shard_map/ppermute | solution.py:17
  321.7 15.0 %copy-start.13 = (pred[512,512]{1,0:T(8,128)(4,1)S(1)}, pred[512,512]{1,0:T(8,128)(4,1)}, u32[]{:S(2)}) copy-start(pred[512,512]{1,0:T(8,128)(4,1)} %fusion.25) | copy-start | bytes 786436
  323.0 4.7 %collective-permute-start.1 = (s32[1]{0:T(128)}, s32[1]{0:T(128)}, u32[]{:S(2)}, u32[]{:S(2)}) collective-permute-start(s32[1]{0:T(128)} %select_n.307), channel_id=1, source_target_pairs={{0,8},{8,16},{16,24},{1,9},{9,17},{17,25},{2,10},{10,18},{18,26},{... | collective-permute-start | bytes 20 | tf_op jit(solution)/shard_map/ppermute | solution.py:17
  331.7 25.1 %collective-permute-start.5 = (f32[16,128,128]{2,1,0:T(8,128)}, f32[16,128,128]{2,1,0:T(8,128)}, u32[]{:S(2)}, u32[]{:S(2)}) collective-permute-start(f32[16,128,128]{2,1,0:T(8,128)} %add_select_fusion.4), channel_id=1, source_target_pairs={{0,8},{8,16},{16,24},{1,9},{9,17},{17,25},{2,10},{10,18},{18,26},{... | collective-permute-start | bytes 3145736 | tf_op jit(solution)/shard_map/ppermute | solution.py:17
  348.0 7.1 %collective-permute-start.2 = (s32[1]{0:T(128)}, s32[1]{0:T(128)}, u32[]{:S(2)}, u32[]{:S(2)}) collective-permute-start(s32[1]{0:T(128)} %select_n.308), channel_id=1, source_target_pairs={{0,8},{8,16},{16,24},{1,9},{9,17},{17,25},{2,10},{10,18},{18,26},{... | collective-permute-start | bytes 20 | tf_op jit(solution)/shard_map/ppermute | solution.py:17
  356.7 2.8 copy-start.4
  359.5 4.1 %copy-start.2 = (bf16[512,2048]{0,1:T(8,128)(2,1)S(1)}, bf16[512,2048]{0,1:T(8,128)(2,1)}, u32[]{:S(2)}) copy-start(bf16[512,2048]{0,1:T(8,128)(2,1)} %copy.113) | copy-start | bytes 6291460
  359.5 4.1 %copy-start.3 = (f32[16,512,128]{1,2,0:T(8,128)S(1)}, f32[16,512,128]{1,2,0:T(8,128)}, u32[]{:S(2)}) copy-start(f32[16,512,128]{1,2,0:T(8,128)} %fusion.5) | copy-start | bytes 12582916
  363.7 2.6 copy-start
  363.7 2.9 copy-start.1
  366.6 4.0 %copy-start.14 = (f32[2048]{0:T(1024)S(1)}, f32[2048]{0:T(1024)}, u32[]{:S(2)}) copy-start(f32[2048]{0:T(1024)} %param.11) | copy-start | bytes 24580
Sparse Core Ops, SparseCore 0:
  57.6 84.7 all-gather.4
  199.3 57.2 all-reduce.5
where the time goes:
time: 399 us; the launch traced here: 397 us
  waiting for transfers between devices  127 us (32%)
  local copies, waits for them, and re-layouts  74.8 us (19%)
  matrix products  44.8 us (11%)
  other arithmetic  39.6 us (10%)
  loops' own time  33.4 us (8%)
  starting transfers between devices  29.5 us (7%)
  between operations  29.4 us (7%)
  blocking collectives  18.5 us (5%)
    all_gather x1, waiting for transfers between devices, entering(): pieces = jax.tree.map(lambda part: lax.all_gather(part, axis), value)  69.7 us
    psum x1, waiting for transfers between devices, spread(): return lax.psum(kept, axis)  57.4 us
    unnamed x45, local copies, waits for them, and re-layouts  35.1 us
    another operation x1, loops' own time, entering(): return lax.fori_loop(0, count - 1, lap, so_far)  33.4 us
    ppermute x6, starting transfers between devices, shifted(): return lax.ppermute(value, axis, pairs)  29.5 us
    dot_general x3, matrix products, direct_part(): jnp.einsum('hqk,khd->qhd', weights, value_rows, preferred_element_type=jn...  29.3 us
    select_n x7, other arithmetic, lap(): jnp.where(position < mine, new, old)  12.2 us
    reshape x3, local copies, waits for them, and re-layouts, finish(): normed.astype(jnp.bfloat16).reshape(query_rows.shape[0], HEADS * HEAD)  10.8 us
  transfers between devices with their start and end apart: 8, of which 2 were waited for; matrix products, arithmetic and copies ran while one was open for 13% of the time, Pallas kernels for 0%

commit v1 on v0

v1 whole, which is shorter than its diff:
```python
import functools

import jax
import jax.numpy as jnp
from jax import lax
from jax.experimental import pallas as pl
from jax.experimental.pallas import tpu as pltpu
from jax.sharding import PartitionSpec as P

HEAD = 128
TILE = 128
BLOCK = 512
HALF_BLOCK = 256
PER = BLOCK // TILE
MESH = pl.DeviceIdType.MESH
F32 = jnp.float32
BF16 = jnp.bfloat16


def dot(a, b, dims):
    return lax.dot_general(a, b, (dims, ((), ())), preferred_element_type=F32)


def rows_below(limit):
    rows = lax.broadcasted_iota(jnp.int32, (TILE, HEAD), 0)
    return (rows < limit).astype(F32).astype(BF16)


def state_kernel(tiles, per_step, doc_ref, fill_ref, key_ref, value_ref, state_ref, mask_ref):
    @pl.when(pl.program_id(0) == 0)
    def _():
        for tile in range(tiles):
            limit = jnp.where(doc_ref[tile] == doc_ref[tiles - 1], fill_ref[tile], 0)
            mask_ref[pl.ds(tile * TILE, TILE), :] = rows_below(limit)

    for head in range(per_step):
        cols = slice(head * HEAD, (head + 1) * HEAD)
        masked = value_ref[:, cols] * mask_ref[...]
        state_ref[cols, :] = dot(key_ref[:, cols], masked, ((0,), (0,)))


def own_state(keys, values, tile_doc, tile_fill):
    length, width = keys.shape
    heads = width // HEAD
    per_step = 2
    block = pl.BlockSpec((length, per_step * HEAD), lambda h: (0, h))
    smem = pl.BlockSpec(memory_space=pltpu.SMEM)
    return pl.pallas_call(
        functools.partial(state_kernel, length // TILE, per_step),
        grid=(heads // per_step,),
        in_specs=[smem, smem, block, block],
        out_specs=pl.BlockSpec((per_step * HEAD, HEAD), lambda h: (h, 0)),
        out_shape=jax.ShapeDtypeStruct((width, HEAD), F32),
        scratch_shapes=[pltpu.VMEM((length, HEAD), BF16)],
        compiler_params=pltpu.CompilerParams(vmem_limit_bytes=32 * 1024 * 1024),
        name="own_state",
    )(tile_doc, tile_fill, keys, values)


def carry_kernel(
    outer, inner, tiles, half,
    doc_ref, state_ref, carry_ref, prev_ref,
    swap_out, swap_in, out1, in1, out3, in3, joined, back_out, back_in,
    swap_sems, send1, recv1, send3, recv3, back_sems,
):
    chips = outer * inner // 2
    part = half // chips
    me = lax.axis_index("outer") * inner + lax.axis_index("inner")
    chip = me // 2
    core = me % 2

    def place(device):
        return (device // inner, device % inner)

    def ahead(k):
        return (chip + k) % chips

    twin = place(chip * 2 + 1 - core)
    barrier = pltpu.get_barrier_semaphore()
    pl.semaphore_signal(barrier, inc=1, device_id=twin, device_id_type=MESH)

    def greet(k, _):
        pl.semaphore_signal(
            barrier, inc=1, device_id=place(ahead(k) * 2 + core), device_id_type=MESH
        )
        return 0

    lax.fori_loop(1, chips, greet, 0)

    my_doc = jnp.full((8, HEAD), doc_ref[tiles - 1], jnp.int32).astype(F32)
    swap_out[pl.ds(0, half), :] = state_ref[pl.ds((1 - core) * half, half), :]
    swap_out[pl.ds(half, 8), :] = my_doc
    pl.semaphore_wait(barrier, chips)

    swap = pltpu.make_async_remote_copy(
        swap_out, swap_in, swap_sems.at[0], swap_sems.at[1], device_id=twin, device_id_type=MESH
    )
    swap.start()
    swap.wait()

    first_core = core == 0
    their_doc = swap_in[pl.ds(half, 8), :]
    doc0 = jnp.where(first_core, my_doc, their_doc)
    doc1 = jnp.where(first_core, their_doc, my_doc)
    keep1 = (doc0 == doc1).astype(F32)[0:1, :]

    def pack(j, _):
        mine = state_ref[pl.ds(core * half + j * part, part), :]
        theirs = swap_in[pl.ds(j * part, part), :]
        state0 = jnp.where(first_core, mine, theirs)
        state1 = jnp.where(first_core, theirs, mine)
        slot = (j - chip + chips) % chips
        out1[slot, pl.ds(0, part), :] = state1 + keep1 * state0
        out1[slot, pl.ds(part, 8), :] = doc1
        return 0

    lax.fori_loop(0, chips, pack, 0)

    def copy1(k):
        return pltpu.make_async_remote_copy(
            out1.at[k], in1.at[k], send1.at[k], recv1.at[k],
            device_id=place(ahead(k) * 2 + core), device_id_type=MESH,
        )

    def copy3(k):
        return pltpu.make_async_remote_copy(
            out3.at[k], in3.at[k], send3.at[k], recv3.at[k],
            device_id=place(ahead(k) * 2 + core), device_id_type=MESH,
        )

    def run(action):
        def step(k, _):
            action(k)
            return 0

        lax.fori_loop(1, chips, step, 0)

    run(lambda k: copy1(k).start())
    in1[0] = out1[0]
    run(lambda k: copy1(k).wait())

    def lap(c, so_far):
        total, doc = so_far
        to = (c - chip + chips) % chips
        slot = (chip - c + chips) % chips
        out3[to, pl.ds(0, part), :] = total
        out3[to, pl.ds(part, 8), :] = doc
        new_doc = in1[slot, pl.ds(part, 8), :]
        keep = (new_doc == doc).astype(F32)[0:1, :]
        return (in1[slot, pl.ds(0, part), :] + keep * total, new_doc)

    lax.fori_loop(
        0, chips, lap, (jnp.zeros((part, HEAD), F32), jnp.full((8, HEAD), -1.0, F32))
    )

    run(lambda k: copy3(k).start())
    in3[0] = out3[0]
    run(lambda k: copy3(k).wait())

    before = in3[0, pl.ds(part, 8), :]
    keep0 = (doc0 == before).astype(F32)[0:1, :]
    prev_ref[...] = jnp.where(first_core, before, doc0)

    def unpack(k, _):
        source = (chip - k + chips) % chips
        entering = in3[k, pl.ds(0, part), :]
        rows = pl.ds(source * part, part)
        mine = state_ref[pl.ds(core * half + source * part, part), :]
        state0 = jnp.where(first_core, mine, swap_in[rows, :])
        between = state0 + keep0 * entering
        joined[rows, :] = jnp.where(first_core, entering, between)
        back_out[rows, :] = jnp.where(first_core, between, entering)
        return 0

    lax.fori_loop(0, chips, unpack, 0)
    back = pltpu.make_async_remote_copy(
        back_out, back_in, back_sems.at[0], back_sems.at[1], device_id=twin, device_id_type=MESH
    )
    back.start()
    carry_ref[pl.ds(core * half, half), :] = joined[...]
    back.wait()
    carry_ref[pl.ds((1 - core) * half, half), :] = back_in[...]


def entering_state(mesh, state, tile_doc):
    outer, inner = mesh.shape["outer"], mesh.shape["inner"]
    chips = outer * inner // 2
    half = state.shape[0] // 2
    part = half // chips
    vmem = pl.BlockSpec(memory_space=pltpu.VMEM)
    slots = pltpu.VMEM((chips, part + 8, HEAD), F32)
    sems = pltpu.SemaphoreType.DMA((chips,))
    pair = pltpu.SemaphoreType.DMA((2,))
    return pl.pallas_call(
        functools.partial(carry_kernel, outer, inner, tile_doc.shape[0], half),
        in_specs=[pl.BlockSpec(memory_space=pltpu.SMEM), vmem],
        out_specs=[vmem, vmem],
        out_shape=[
            jax.ShapeDtypeStruct(state.shape, F32),
            jax.ShapeDtypeStruct((8, HEAD), F32),
        ],
        scratch_shapes=[
            pltpu.VMEM((half + 8, HEAD), F32),
            pltpu.VMEM((half + 8, HEAD), F32),
            slots, slots, slots, slots,
            pltpu.VMEM((half, HEAD), F32),
            pltpu.VMEM((half, HEAD), F32),
            pltpu.VMEM((half, HEAD), F32),
            pair, sems, sems, sems, sems, pair,
        ],
        compiler_params=pltpu.CompilerParams(
            collective_id=0, has_side_effects=True, vmem_limit_bytes=32 * 1024 * 1024
        ),
        name="entering_state",
    )(tile_doc, state)


def split(value):
    high = value.astype(BF16)
    return high, (value - high.astype(F32)).astype(BF16)


def attend_kernel(
    tiles, per_step,
    doc_ref, fill_ref, prev_ref, query_ref, key_ref, value_ref, carry_ref, gain_ref, out_ref,
    real_ref, last_ref, uses_ref, pair_ref,
):
    blocks = tiles // PER

    @pl.when(pl.program_id(0) == 0)
    def _():
        entering = prev_ref[0:1, :]
        for tile in range(tiles):
            block = tile // PER
            rows = pl.ds(tile * TILE, TILE)
            doc = doc_ref[tile]
            real = rows_below(fill_ref[tile])
            real_ref[rows, :] = real
            last_ref[rows, :] = rows_below(
                jnp.where(doc == doc_ref[block * PER + PER - 1], fill_ref[tile], 0)
            )
            if block == 0:
                same = (jnp.full((1, HEAD), doc, jnp.int32).astype(F32) == entering).astype(F32)
                uses_ref[rows, :] = (real.astype(F32) * same).astype(BF16)
            else:
                uses_ref[rows, :] = rows_below(
                    jnp.where(doc == doc_ref[block * PER - 1], fill_ref[tile], 0)
                )
        above = lax.broadcasted_iota(jnp.int32, (TILE, TILE), 0)
        across = lax.broadcasted_iota(jnp.int32, (TILE, TILE), 1)
        lower = (above >= across).astype(F32).astype(BF16)
        for block in range(blocks):
            for i in range(PER):
                for j in range(PER):
                    spot = (block, slice(i * TILE, (i + 1) * TILE), slice(j * TILE, (j + 1) * TILE))
                    if j > i:
                        pair_ref[spot] = jnp.zeros((TILE, TILE), BF16)
                    elif j == i:
                        pair_ref[spot] = lower
                    else:
                        same = doc_ref[block * PER + i] == doc_ref[block * PER + j]
                        pair_ref[spot] = rows_below(jnp.where(same, TILE, 0))

    for head in range(per_step):
        cols = slice(head * HEAD, (head + 1) * HEAD)
        gain = gain_ref[:, cols]
        carry = carry_ref[cols, :]
        for block in range(blocks):
            rows = slice(block * BLOCK, (block + 1) * BLOCK)
            query = query_ref[rows, cols] * real_ref[rows, :]
            key = key_ref[rows, cols]
            plain = value_ref[rows, cols]
            value = plain * real_ref[rows, :]
            high, low = split(carry)
            for part in range(BLOCK // HALF_BLOCK):
                begin = part * HALF_BLOCK
                end = begin + HALF_BLOCK
                scores = dot(query[begin:end], key[:end], ((1,), (1,)))
                weights = scores.astype(BF16) * pair_ref[block, begin:end, :end]
                raw = dot(weights, value[:end], ((1,), (0,)))
                place = slice(block * BLOCK + begin, block * BLOCK + end)
                using = query[begin:end] * uses_ref[place, :]
                raw = raw + (dot(using, high, ((1,), (0,))) + dot(using, low, ((1,), (0,))))
                meansq = jnp.mean(raw * raw, axis=-1, keepdims=True)
                normed = raw * lax.rsqrt(meansq + 1e-06) * gain
                out_ref[place, cols] = normed.astype(BF16)
            if block < blocks - 1:
                own = dot(key, plain * last_ref[rows, :], ((0,), (0,)))
                closing = doc_ref[block * PER + PER - 1]
                if block == 0:
                    closing = jnp.full((1, HEAD), closing, jnp.int32).astype(F32)
                    keep = (closing == prev_ref[0:1, :]).astype(F32)
                else:
                    keep = (closing == doc_ref[block * PER - 1]).astype(F32)
                carry = own + keep * carry


def attend(queries, keys, values, gain, tile_doc, tile_fill, carry, prev):
    length, width = queries.shape
    heads = width // HEAD
    per_step = 2
    block = pl.BlockSpec((length, per_step * HEAD), lambda h: (0, h))
    smem = pl.BlockSpec(memory_space=pltpu.SMEM)
    mask = pltpu.VMEM((length, HEAD), BF16)
    return pl.pallas_call(
        functools.partial(attend_kernel, length // TILE, per_step),
        grid=(heads // per_step,),
        in_specs=[
            smem,
            smem,
            pl.BlockSpec((8, HEAD), lambda h: (0, 0)),
            block,
            block,
            block,
            pl.BlockSpec((per_step * HEAD, HEAD), lambda h: (h, 0)),
            pl.BlockSpec((1, per_step * HEAD), lambda h: (0, h)),
        ],
        out_specs=block,
        out_shape=jax.ShapeDtypeStruct((length, width), BF16),
        scratch_shapes=[mask, mask, mask, pltpu.VMEM((length // BLOCK, BLOCK, BLOCK), BF16)],
        compiler_params=pltpu.CompilerParams(vmem_limit_bytes=48 * 1024 * 1024),
        name="attend",
    )(tile_doc, tile_fill, prev, queries, keys, values, carry, gain.reshape(1, width))


def solution(mesh):
    def body(queries, keys, values, gain, tile_doc, tile_fill):
        state = own_state(keys, values, tile_doc, tile_fill)
        carry, prev = entering_state(mesh, state, tile_doc)
        return attend(queries, keys, values, gain, tile_doc, tile_fill, carry, prev)

    rows = P(("outer", "inner"), None)
    tiles = P(("outer", "inner"))
    return jax.shard_map(
        body, mesh=mesh, in_specs=(rows, rows, rows, P(), tiles, tiles), out_specs=rows,
        check_vma=False,
    )
```

time: 399 us -> 78.5 us (0.20)
  waiting for transfers between devices: 127 us -> 0 us
  Pallas kernels: 0 us -> 71.3 us
  local copies, waits for them, and re-layouts: 74.8 us -> 6.89 us
  matrix products: 44.8 us -> 0 us
  other arithmetic: 39.6 us -> 0 us
  loops' own time: 33.4 us -> 0 us
  starting transfers between devices: 29.5 us -> 0 us
  between operations: 29.4 us -> 0.05 us
  blocking collectives: 18.5 us -> 0 us
    pallas_call x0 -> x3, Pallas kernels: none -> 71.3 us  [the longest x1 40.3 us: entering_state(): pl.pallas_call(functools.partial(carry_kernel, outer, inner, tile_doc.sha...]
    all_gather x1 -> x0, waiting for transfers between devices: 69.7 us -> none  [entering(): pieces = jax.tree.map(lambda part: lax.all_gather(part, axis), value)]
    psum x1 -> x0, waiting for transfers between devices: 57.4 us -> none  [spread(): return lax.psum(kept, axis)]
    dot_general x9 -> x0, matrix products: 44.8 us -> none  [the longest x3 29.3 us: direct_part(): jnp.einsum('hqk,khd->qhd', weights, value_rows, preferred_element_type=jn...]
    another operation x1 -> x0, loops' own time: 33.4 us -> none  [entering(): return lax.fori_loop(0, count - 1, lap, so_far)]
    ppermute x6 -> x0, starting transfers between devices: 29.5 us -> none  [shifted(): return lax.ppermute(value, axis, pairs)]
    unnamed x45 -> x14, local copies, waits for them, and re-layouts: 35.1 us -> 6.89 us
    slice x10 -> x0, local copies, waits for them, and re-layouts: 24.1 us -> none  [the longest x2 9.74 us: body(): value_all[lower:upper]]
  transfers between devices with their start and end apart: 8 -> 0, of which waited for: 2 -> 0; matrix products, arithmetic and copies ran while one was open for 13% -> 0% of each run, Pallas kernels for 0% -> 0%
where the time goes in v1:
time: 78.5 us; the launch traced here: 78.3 us
  Pallas kernels  71.3 us (91%)
  local copies, waits for them, and re-layouts  6.89 us (9%)
    pallas_call x1, Pallas kernels, entering_state(): pl.pallas_call(functools.partial(carry_kernel, outer, inner, tile_doc.sha...  40.3 us
    pallas_call x1, Pallas kernels, attend(): pl.pallas_call(functools.partial(attend_kernel, length // TILE, per_step)...  25.3 us
    unnamed x14, local copies, waits for them, and re-layouts  6.89 us
    pallas_call x1, Pallas kernels, own_state(): pl.pallas_call(functools.partial(state_kernel, length // TILE, per_step),...  5.75 us

profile of v1, /device:TPU:0, one launch (start us, length us, event | category | flops | bytes accessed | tf_op | source)
XLA Modules:
  0.0 78.3 jit_solution(2875555941534870893)
XLA Ops:
  0.0 0.0 copy-start
  0.0 2.8 %copy-done = bf16[1536,2048]{1,0:T(8,128)(2,1)S(1)} copy-done((bf16[1536,2048]{1,0:T(8,128)(2,1)S(1)}, bf16[1536,2048]{1,0:T(8,128)(2,1)}, u32[]{:S(2)}) %copy-start) | copy-done | bytes 6291480
  2.8 0.0 copy-start.1
  2.8 2.8 %copy-done.1 = bf16[1536,2048]{1,0:T(8,128)(2,1)S(1)} copy-done((bf16[1536,2048]{1,0:T(8,128)(2,1)S(1)}, bf16[1536,2048]{1,0:T(8,128)(2,1)}, u32[]{:S(2)}) %copy-start.1) | copy-done | bytes 6291480
  5.6 0.0 copy-start.3
  5.6 0.7 copy-done.3
  6.2 0.0 copy-start.5
  6.2 0.7 copy-done.5
  6.9 0.0 copy-start.2
  6.9 0.0 copy-start.4
  6.9 0.0 copy-start.6
  6.9 5.8 %own_state.1.state_ref = f32[2048,128]{1,0:T(8,128)S(1)} custom-call(s32[12]{0:T(128)S(1)} %copy-done.3, s32[12]{0:T(128)S(1)} %copy-done.5, bf16[1536,2048]{1,0:T(8,128)(2,1)S(1)} %copy-done, bf16[1536,2048]{1,0:T(8,128)(2,1)S(1)} %copy-done.1), custom_call_target="tpu_custom_call" | custom-call | tf_op jit(solution)/shard_map/own_state/pallas_call | solution.py:48
  12.6 40.3 %entering_state.1 = (f32[2048,128]{1,0:T(8,128)S(1)}, f32[8,128]{1,0:T(8,128)S(1)}) custom-call(s32[12]{0:T(128)S(1)} %copy-done.3, f32[2048,128]{1,0:T(8,128)S(1)} %own_state.1.state_ref), custom_call_target="tpu_custom_call" | custom-call | tf_op jit(solution)/shard_map/entering_state/pallas_call | solution.py:194
  52.9 0.0 copy-done.2
  52.9 0.0 copy-done.4
  53.0 0.0 copy-done.6
  53.0 25.3 %attend.1 = bf16[1536,2048]{1,0:T(8,128)(2,1)} custom-call(s32[12]{0:T(128)S(1)} %copy-done.4, s32[12]{0:T(128)S(1)} %copy-done.6, f32[8,128]{1,0:T(8,128)S(1)} %get-tuple-element.7.prev_ref, bf16[1536,2048]{1,0:T(8,128)(2,1)} %query_ref.1, bf16[1536,2048]{1,0:T(8,128)(2,1)} %key_ref.3, bf16[1536,2048]{1,0:T(8,128)(2,1)} %value_ref.3, ...), custom_call_target="tpu_custom_call" | custom-call | tf_op jit(solution)/shard_map/attend/pallas_call | solution.py:305
Async XLA Ops:
  0.0 2.8 %copy-start = (bf16[1536,2048]{1,0:T(8,128)(2,1)S(1)}, bf16[1536,2048]{1,0:T(8,128)(2,1)}, u32[]{:S(2)}) copy-start(bf16[1536,2048]{1,0:T(8,128)(2,1)} %key_ref.3) | copy-start | bytes 18874372
  2.8 2.8 %copy-start.1 = (bf16[1536,2048]{1,0:T(8,128)(2,1)S(1)}, bf16[1536,2048]{1,0:T(8,128)(2,1)}, u32[]{:S(2)}) copy-start(bf16[1536,2048]{1,0:T(8,128)(2,1)} %value_ref.3) | copy-start | bytes 18874372
  5.6 0.7 copy-start.3
  6.2 0.7 copy-start.5
  6.9 46.0 %copy-start.2 = (f32[2048]{0:T(1024)S(1)}, f32[2048]{0:T(1024)}, u32[]{:S(2)}) copy-start(f32[2048]{0:T(1024)} %param.9) | copy-start | bytes 24580
  6.9 46.1 %copy-start.4 = (s32[12]{0:T(128)S(1)}, s32[12]{0:T(128)}, u32[]{:S(2)}) copy-start(s32[12]{0:T(128)} %doc_ref.5) | copy-start | bytes 148
  6.9 46.1 %copy-start.6 = (s32[12]{0:T(128)S(1)}, s32[12]{0:T(128)}, u32[]{:S(2)}) copy-start(s32[12]{0:T(128)} %fill_ref.3) | copy-start | bytes 148

commit v2 on v1

v2 whole, which is shorter than its diff:
```python
import functools

import jax
import jax.numpy as jnp
from jax import lax
from jax.experimental import pallas as pl
from jax.experimental.pallas import tpu as pltpu
from jax.sharding import PartitionSpec as P

HEAD = 128
TILE = 128
BLOCK = 512
HALF_BLOCK = 256
PER = BLOCK // TILE
MESH = pl.DeviceIdType.MESH
F32 = jnp.float32
BF16 = jnp.bfloat16


def dot(a, b, dims):
    return lax.dot_general(a, b, (dims, ((), ())), preferred_element_type=F32)


def rows_below(limit):
    rows = lax.broadcasted_iota(jnp.int32, (TILE, HEAD), 0)
    return (rows < limit).astype(F32).astype(BF16)


def split(value):
    high = value.astype(BF16)
    return high, (value - high.astype(F32)).astype(BF16)


def build_masks(tiles, doc_ref, fill_ref, real_ref, last_ref, uses_ref, pair_ref):
    for tile in range(tiles):
        block = tile // PER
        rows = pl.ds(tile * TILE, TILE)
        doc = doc_ref[tile]
        fill = fill_ref[tile]
        real_ref[rows, :] = rows_below(fill)
        closing = doc_ref[block * PER + PER - 1]
        last_ref[rows, :] = rows_below(jnp.where(doc == closing, fill, 0))
        if block > 0:
            opening = doc_ref[block * PER - 1]
            uses_ref[rows, :] = rows_below(jnp.where(doc == opening, fill, 0))
    above = lax.broadcasted_iota(jnp.int32, (TILE, TILE), 0)
    across = lax.broadcasted_iota(jnp.int32, (TILE, TILE), 1)
    lower = (above >= across).astype(F32).astype(BF16)
    for block in range(tiles // PER):
        for i in range(PER):
            for j in range(PER):
                spot = (block, pl.ds(i * TILE, TILE), pl.ds(j * TILE, TILE))
                if j > i:
                    pair_ref[spot] = jnp.zeros((TILE, TILE), BF16)
                elif j == i:
                    pair_ref[spot] = lower
                else:
                    same = doc_ref[block * PER + i] == doc_ref[block * PER + j]
                    pair_ref[spot] = rows_below(jnp.where(same, TILE, 0))


def local_kernel(
    outer, inner, tiles, heads, chunks,
    doc_ref, fill_ref, query_hbm, key_hbm, value_hbm, raw_hbm, carry_ref, prev_ref,
    query_ref, key_ref, value_ref, raw_ref, state_ref,
    real_ref, last_ref, uses_ref, pair_ref,
    swap_out, swap_in, out1, in1, out3, in3, back_out, back_in,
    load_sems, store_sems, swap_sems, send1, recv1, send3, recv3, back_sems,
):
    blocks = tiles // PER
    half = heads * HEAD // 2
    chips = outer * inner // 2
    part = half // chips
    me = lax.axis_index("outer") * inner + lax.axis_index("inner")
    chip = me // 2
    core = me % 2
    wide = heads * HEAD // chunks
    per_chunk = heads // chunks

    def place(device):
        return (device // inner, device % inner)

    def ahead(k):
        return (chip + k) % chips

    def chunk_at(c):
        return ((1 - core) * (chunks // 2) + c) % chunks

    def load(array, c):
        source = (key_hbm, value_hbm, query_hbm)[array]
        target = (key_ref, value_ref, query_ref)[array]
        index = c if array == 2 else chunk_at(c)
        cols = pl.ds(pl.multiple_of(index * wide, wide), wide)
        return pltpu.make_async_copy(
            source.at[:, cols], target.at[:, cols], load_sems.at[array, c]
        )

    for c in range(chunks):
        load(0, c).start()
        load(1, c).start()
    for c in range(chunks):
        load(2, c).start()

    twin = place(chip * 2 + 1 - core)
    barrier = pltpu.get_barrier_semaphore()
    pl.semaphore_signal(barrier, inc=1, device_id=twin, device_id_type=MESH)

    def greet(k, _):
        pl.semaphore_signal(
            barrier, inc=1, device_id=place(ahead(k) * 2 + core), device_id_type=MESH
        )
        return 0

    lax.fori_loop(1, chips, greet, 0)

    build_masks(tiles, doc_ref, fill_ref, real_ref, last_ref, uses_ref, pair_ref)

    def joins(block):
        closing = doc_ref[block * PER + PER - 1]
        return (closing == doc_ref[block * PER - 1]).astype(F32)

    def columns(head):
        return pl.ds(pl.multiple_of(head * HEAD, HEAD), HEAD)

    def added(head, block):
        rows = pl.ds(block * BLOCK, BLOCK)
        cols = columns(head)
        masked = value_ref[rows, cols] * last_ref[rows, :]
        return dot(key_ref[rows, cols], masked, ((0,), (0,)))

    def summed(c):
        load(0, c).wait()
        load(1, c).wait()

        def step(i, _):
            head = chunk_at(c) * per_chunk + i
            total = added(head, 0)
            for block in range(1, blocks):
                total = added(head, block) + joins(block) * total
            state_ref[columns(head), :] = total
            return 0

        lax.fori_loop(0, per_chunk, step, 0)

    for c in range(chunks // 2):
        summed(c)
    my_doc = jnp.full((8, HEAD), doc_ref[tiles - 1], jnp.int32).astype(F32)
    swap_out[pl.ds(0, half), :] = state_ref[pl.ds((1 - core) * half, half), :]
    swap_out[pl.ds(half, 8), :] = my_doc
    pl.semaphore_wait(barrier, chips)
    swap = pltpu.make_async_remote_copy(
        swap_out, swap_in, swap_sems.at[0], swap_sems.at[1], device_id=twin, device_id_type=MESH
    )
    swap.start()
    for c in range(chunks // 2, chunks):
        summed(c)
    swap.wait()

    first_core = core == 0
    their_doc = swap_in[pl.ds(half, 8), :]
    doc0 = jnp.where(first_core, my_doc, their_doc)
    doc1 = jnp.where(first_core, their_doc, my_doc)
    keep1 = (doc0 == doc1).astype(F32)[0:1, :]

    def pack(j, _):
        mine = state_ref[pl.ds(core * half + j * part, part), :]
        theirs = swap_in[pl.ds(j * part, part), :]
        state0 = jnp.where(first_core, mine, theirs)
        state1 = jnp.where(first_core, theirs, mine)
        slot = (j - chip + chips) % chips
        out1[slot, pl.ds(0, part), :] = state1 + keep1 * state0
        out1[slot, pl.ds(part, 8), :] = doc1
        return 0

    lax.fori_loop(0, chips, pack, 0)

    def copy1(k):
        return pltpu.make_async_remote_copy(
            out1.at[k], in1.at[k], send1.at[k], recv1.at[k],
            device_id=place(ahead(k) * 2 + core), device_id_type=MESH,
        )

    def copy3(k):
        return pltpu.make_async_remote_copy(
            out3.at[k], in3.at[k], send3.at[k], recv3.at[k],
            device_id=place(ahead(k) * 2 + core), device_id_type=MESH,
        )

    def run(begin, end, action):
        def step(k, _):
            action(k)
            return 0

        lax.fori_loop(begin, end, step, 0)

    def store(head):
        cols = columns(head)
        return pltpu.make_async_copy(raw_ref.at[:, cols], raw_hbm.at[:, cols], store_sems.at[head])

    def local(head):
        cols = columns(head)
        carry = None
        for block in range(blocks):
            rows = pl.ds(block * BLOCK, BLOCK)
            query = query_ref[rows, cols] * real_ref[rows, :]
            key = key_ref[rows, cols]
            value = value_ref[rows, cols] * real_ref[rows, :]
            if block > 0:
                high, low = split(carry)
            for piece in range(BLOCK // HALF_BLOCK):
                begin = piece * HALF_BLOCK
                end = begin + HALF_BLOCK
                at = pl.ds(block * BLOCK + begin, HALF_BLOCK)
                scores = dot(query[begin:end], key[:end], ((1,), (1,)))
                keep = pair_ref[block, pl.ds(begin, HALF_BLOCK), pl.ds(0, end)]
                raw = dot(scores.astype(BF16) * keep, value[:end], ((1,), (0,)))
                if block > 0:
                    using = query[begin:end] * uses_ref[at, :]
                    raw = raw + (dot(using, high, ((1,), (0,))) + dot(using, low, ((1,), (0,))))
                raw_ref[at, cols] = raw
            if block < blocks - 1:
                fresh = added(head, block)
                carry = fresh if block == 0 else fresh + joins(block) * carry
        store(head).start()

    run(1, chips, lambda k: copy1(k).start())
    in1[0] = out1[0]
    for c in range(chunks):
        load(2, c).wait()
    run(0, heads // 2, local)
    run(1, chips, lambda k: copy1(k).wait())

    def lap(c, so_far):
        total, doc = so_far
        to = (c - chip + chips) % chips
        slot = (chip - c + chips) % chips
        out3[to, pl.ds(0, part), :] = total
        out3[to, pl.ds(part, 8), :] = doc
        new_doc = in1[slot, pl.ds(part, 8), :]
        keep = (new_doc == doc).astype(F32)[0:1, :]
        return (in1[slot, pl.ds(0, part), :] + keep * total, new_doc)

    lax.fori_loop(
        0, chips, lap, (jnp.zeros((part, HEAD), F32), jnp.full((8, HEAD), -1.0, F32))
    )

    run(1, chips, lambda k: copy3(k).start())
    in3[0] = out3[0]
    run(heads // 2, heads, local)
    run(1, chips, lambda k: copy3(k).wait())

    before = in3[0, pl.ds(part, 8), :]
    keep0 = (doc0 == before).astype(F32)[0:1, :]
    prev_ref[...] = jnp.where(first_core, before, doc0)

    def unpack(k, _):
        source = (chip - k + chips) % chips
        entering = in3[k, pl.ds(0, part), :]
        rows = pl.ds(source * part, part)
        own_rows = pl.ds(core * half + source * part, part)
        state0 = jnp.where(first_core, state_ref[own_rows, :], swap_in[rows, :])
        between = state0 + keep0 * entering
        carry_ref[own_rows, :] = jnp.where(first_core, entering, between)
        back_out[rows, :] = jnp.where(first_core, between, entering)
        return 0

    lax.fori_loop(0, chips, unpack, 0)
    back = pltpu.make_async_remote_copy(
        back_out, back_in, back_sems.at[0], back_sems.at[1], device_id=twin, device_id_type=MESH
    )
    back.start()
    run(0, heads, lambda head: store(head).wait())
    back.wait()
    carry_ref[pl.ds((1 - core) * half, half), :] = back_in[...]


def local_part(mesh, queries, keys, values, tile_doc, tile_fill):
    outer, inner = mesh.shape["outer"], mesh.shape["inner"]
    length, width = queries.shape
    heads = width // HEAD
    chunks = 4
    chips = outer * inner // 2
    half = width // 2
    part = half // chips
    vmem = pl.BlockSpec(memory_space=pltpu.VMEM)
    smem = pl.BlockSpec(memory_space=pltpu.SMEM)
    hbm = pl.BlockSpec(memory_space=pl.ANY)
    slots = pltpu.VMEM((chips, part + 8, HEAD), F32)
    halves = pltpu.VMEM((half, HEAD), F32)
    swaps = pltpu.VMEM((half + 8, HEAD), F32)
    rows = pltpu.VMEM((length, width), BF16)
    mask = pltpu.VMEM((length, HEAD), BF16)
    sems = pltpu.SemaphoreType.DMA((chips,))
    pair = pltpu.SemaphoreType.DMA((2,))
    return pl.pallas_call(
        functools.partial(local_kernel, outer, inner, length // TILE, heads, chunks),
        in_specs=[smem, smem, hbm, hbm, hbm],
        out_specs=[hbm, vmem, vmem],
        out_shape=[
            jax.ShapeDtypeStruct((length, width), F32),
            jax.ShapeDtypeStruct((width, HEAD), F32),
            jax.ShapeDtypeStruct((8, HEAD), F32),
        ],
        scratch_shapes=[
            rows, rows, rows,
            pltpu.VMEM((length, width), F32),
            pltpu.VMEM((width, HEAD), F32),
            mask, mask, mask,
            pltpu.VMEM((length // BLOCK, BLOCK, BLOCK), BF16),
            swaps, swaps, slots, slots, slots, slots, halves, halves,
            pltpu.SemaphoreType.DMA((3, chunks)),
            pltpu.SemaphoreType.DMA((heads,)),
            pair, sems, sems, sems, sems, pair,
        ],
        compiler_params=pltpu.CompilerParams(
            collective_id=0, has_side_effects=True, vmem_limit_bytes=56 * 1024 * 1024
        ),
        name="local_part",
    )(tile_doc, tile_fill, queries, keys, values)


def finish_kernel(
    tiles, per_step,
    doc_ref, fill_ref, prev_ref, query_ref, raw_ref, carry_ref, gain_ref, out_ref, uses_ref,
):
    @pl.when(pl.program_id(0) == 0)
    def _():
        entering = prev_ref[0:1, :]
        for tile in range(tiles):
            doc = jnp.full((1, HEAD), doc_ref[tile], jnp.int32).astype(F32)
            same = (doc == entering).astype(F32)
            real = rows_below(fill_ref[tile]).astype(F32)
            uses_ref[pl.ds(tile * TILE, TILE), :] = (real * same).astype(BF16)

    for head in range(per_step):
        cols = slice(head * HEAD, (head + 1) * HEAD)
        high, low = split(carry_ref[cols, :])
        using = query_ref[:, cols] * uses_ref[...]
        raw = raw_ref[:, cols]
        raw = raw + (dot(using, high, ((1,), (0,))) + dot(using, low, ((1,), (0,))))
        meansq = jnp.mean(raw * raw, axis=-1, keepdims=True)
        out_ref[:, cols] = (raw * lax.rsqrt(meansq + 1e-06) * gain_ref[:, cols]).astype(BF16)


def finish(queries, raw, gain, tile_doc, tile_fill, carry, prev):
    length, width = queries.shape
    heads = width // HEAD
    per_step = 2
    block = pl.BlockSpec((length, per_step * HEAD), lambda h: (0, h))
    smem = pl.BlockSpec(memory_space=pltpu.SMEM)
    return pl.pallas_call(
        functools.partial(finish_kernel, length // TILE, per_step),
        grid=(heads // per_step,),
        in_specs=[
            smem,
            smem,
            pl.BlockSpec((8, HEAD), lambda h: (0, 0)),
            block,
            block,
            pl.BlockSpec((per_step * HEAD, HEAD), lambda h: (h, 0)),
            pl.BlockSpec((1, per_step * HEAD), lambda h: (0, h)),
        ],
        out_specs=block,
        out_shape=jax.ShapeDtypeStruct((length, width), BF16),
        scratch_shapes=[pltpu.VMEM((length, HEAD), BF16)],
        compiler_params=pltpu.CompilerParams(vmem_limit_bytes=56 * 1024 * 1024),
        name="finish",
    )(tile_doc, tile_fill, prev, queries, raw, carry, gain.reshape(1, width))


def solution(mesh):
    def body(queries, keys, values, gain, tile_doc, tile_fill):
        raw, carry, prev = local_part(mesh, queries, keys, values, tile_doc, tile_fill)
        return finish(queries, raw, gain, tile_doc, tile_fill, carry, prev)

    rows = P(("outer", "inner"), None)
    tiles = P(("outer", "inner"))
    return jax.shard_map(
        body, mesh=mesh, in_specs=(rows, rows, rows, P(), tiles, tiles), out_specs=rows,
        check_vma=False,
    )
```

time: 78.5 us -> 58.6 us (0.75)
  Pallas kernels: 71.3 us -> 58.4 us
  local copies, waits for them, and re-layouts: 6.89 us -> 0 us
    pallas_call x3 -> x2, Pallas kernels: 71.3 us -> 58.4 us  [the longest x1 44.2 us: local_part(): pl.pallas_call(functools.partial(local_kernel, outer, inner, length // TI...]
    unnamed x14 -> x0, local copies, waits for them, and re-layouts: 6.89 us -> none
where the time goes in v2:
time: 58.6 us; the launch traced here: 58.4 us
  Pallas kernels  58.4 us (100%)
    pallas_call x1, Pallas kernels, local_part(): pl.pallas_call(functools.partial(local_kernel, outer, inner, length // TI...  44.2 us
    pallas_call x1, Pallas kernels, finish(): pl.pallas_call(functools.partial(finish_kernel, length // TILE, per_step)...  14.3 us

profile of v2, /device:TPU:0, one launch (start us, length us, event | category | flops | bytes accessed | tf_op | source)
XLA Modules:
  0.0 58.4 jit_solution(7143562551573790520)
XLA Ops:
  0.0 44.2 %local_part.1 = (f32[1536,2048]{1,0:T(8,128)}, f32[2048,128]{1,0:T(8,128)}, f32[8,128]{1,0:T(8,128)}) custom-call(s32[12]{0:T(128)} %doc_ref.3, s32[12]{0:T(128)} %fill_ref.3, bf16[1536,2048]{1,0:T(8,128)(2,1)} %query_ref.1, bf16[1536,2048]{1,0:T(8,128)(2,1)} %key_hbm.1, bf16[1536,2048]{1,0:T(8,128)(2,1)} %value_hbm.1), custom_call_target="tpu_custom_call" | custom-call | tf_op jit(solution)/shard_map/local_part/pallas_call | solution.py:295
  44.2 14.3 %finish.1 = bf16[1536,2048]{1,0:T(8,128)(2,1)} custom-call(s32[12]{0:T(128)} %doc_ref.3, s32[12]{0:T(128)} %fill_ref.3, f32[8,128]{1,0:T(8,128)} %get-tuple-element.8.prev_ref, bf16[1536,2048]{1,0:T(8,128)(2,1)} %query_ref.1, f32[1536,2048]{1,0:T(8,128)} %get-tuple-element.9.raw_ref, f32[2048,128]{1,0:T(8,128)} %get-tuple-element.10.carry_ref, f32[1,2048]{1,0:T(1,128)} %bitcast.1), custom_call_target="tpu_custom_call" | custom-call | tf_op jit(solution)/shard_map/finish/pallas_call | solution.py:351

commit v3 on v2

--- a/solution.py
+++ b/solution.py
@@ -28,7 +28,7 @@
 
 def split(value):
     high = value.astype(BF16)
-    return high, (value - high.astype(F32)).astype(BF16)
+    return jnp.concatenate([high, (value - high.astype(F32)).astype(BF16)], axis=0)
 
 
 def build_masks(tiles, doc_ref, fill_ref, real_ref, last_ref, uses_ref, pair_ref):
@@ -61,11 +61,11 @@
 
 def local_kernel(
     outer, inner, tiles, heads, chunks,
-    doc_ref, fill_ref, query_hbm, key_hbm, value_hbm, raw_hbm, carry_ref, prev_ref,
-    query_ref, key_ref, value_ref, raw_ref, state_ref,
+    doc_ref, fill_ref, query_hbm, key_hbm, value_hbm, raw_ref, query_ref, carry_ref, prev_ref,
+    key_ref, value_ref, state_ref,
     real_ref, last_ref, uses_ref, pair_ref,
     swap_out, swap_in, out1, in1, out3, in3, back_out, back_in,
-    load_sems, store_sems, swap_sems, send1, recv1, send3, recv3, back_sems,
+    load_sems, swap_sems, send1, recv1, send3, recv3, back_sems,
 ):
     blocks = tiles // PER
     half = heads * HEAD // 2
@@ -193,10 +193,6 @@
 
         lax.fori_loop(begin, end, step, 0)
 
-    def store(head):
-        cols = columns(head)
-        return pltpu.make_async_copy(raw_ref.at[:, cols], raw_hbm.at[:, cols], store_sems.at[head])
-
     def local(head):
         cols = columns(head)
         carry = None
@@ -206,7 +202,7 @@
             key = key_ref[rows, cols]
             value = value_ref[rows, cols] * real_ref[rows, :]
             if block > 0:
-                high, low = split(carry)
+                parts = split(carry)
             for piece in range(BLOCK // HALF_BLOCK):
                 begin = piece * HALF_BLOCK
                 end = begin + HALF_BLOCK
@@ -216,12 +212,12 @@
                 raw = dot(scores.astype(BF16) * keep, value[:end], ((1,), (0,)))
                 if block > 0:
                     using = query[begin:end] * uses_ref[at, :]
-                    raw = raw + (dot(using, high, ((1,), (0,))) + dot(using, low, ((1,), (0,))))
+                    twice = jnp.concatenate([using, using], axis=1)
+                    raw = raw + dot(twice, parts, ((1,), (0,)))
                 raw_ref[at, cols] = raw
             if block < blocks - 1:
                 fresh = added(head, block)
                 carry = fresh if block == 0 else fresh + joins(block) * carry
-        store(head).start()
 
     run(1, chips, lambda k: copy1(k).start())
     in1[0] = out1[0]
@@ -269,7 +265,6 @@
         back_out, back_in, back_sems.at[0], back_sems.at[1], device_id=twin, device_id_type=MESH
     )
     back.start()
-    run(0, heads, lambda head: store(head).wait())
     back.wait()
     carry_ref[pl.ds((1 - core) * half, half), :] = back_in[...]
 
@@ -295,25 +290,24 @@
     return pl.pallas_call(
         functools.partial(local_kernel, outer, inner, length // TILE, heads, chunks),
         in_specs=[smem, smem, hbm, hbm, hbm],
-        out_specs=[hbm, vmem, vmem],
+        out_specs=[vmem, vmem, vmem, vmem],
         out_shape=[
-            jax.ShapeDtypeStruct((length, width), F32),
+            pltpu.VMEM((length, width), F32),
+            pltpu.VMEM((length, width), BF16),
             jax.ShapeDtypeStruct((width, HEAD), F32),
             jax.ShapeDtypeStruct((8, HEAD), F32),
         ],
         scratch_shapes=[
-            rows, rows, rows,
-            pltpu.VMEM((length, width), F32),
+            rows, rows,
             pltpu.VMEM((width, HEAD), F32),
             mask, mask, mask,
             pltpu.VMEM((length // BLOCK, BLOCK, BLOCK), BF16),
             swaps, swaps, slots, slots, slots, slots, halves, halves,
             pltpu.SemaphoreType.DMA((3, chunks)),
-            pltpu.SemaphoreType.DMA((heads,)),
             pair, sems, sems, sems, sems, pair,
         ],
         compiler_params=pltpu.CompilerParams(
-            collective_id=0, has_side_effects=True, vmem_limit_bytes=56 * 1024 * 1024
+            collective_id=0, has_side_effects=True, vmem_limit_bytes=34 * 1024 * 1024
         ),
         name="local_part",
     )(tile_doc, tile_fill, queries, keys, values)
@@ -334,10 +328,12 @@
 
     for head in range(per_step):
         cols = slice(head * HEAD, (head + 1) * HEAD)
-        high, low = split(carry_ref[cols, :])
-        using = query_ref[:, cols] * uses_ref[...]
-        raw = raw_ref[:, cols]
-        raw = raw + (dot(using, high, ((1,), (0,))) + dot(using, low, ((1,), (0,))))
+        begin = (pl.program_id(0) * per_step + head) * HEAD
+        here = pl.ds(pl.multiple_of(begin, HEAD), HEAD)
+        using = query_ref[:, here] * uses_ref[...]
+        twice = jnp.concatenate([using, using], axis=1)
+        raw = raw_ref[:, here]
+        raw = raw + dot(twice, split(carry_ref[cols, :]), ((1,), (0,)))
         meansq = jnp.mean(raw * raw, axis=-1, keepdims=True)
         out_ref[:, cols] = (raw * lax.rsqrt(meansq + 1e-06) * gain_ref[:, cols]).astype(BF16)
 
@@ -355,23 +351,23 @@
             smem,
             smem,
             pl.BlockSpec((8, HEAD), lambda h: (0, 0)),
-            block,
-            block,
+            pl.BlockSpec(memory_space=pltpu.VMEM),
+            pl.BlockSpec(memory_space=pltpu.VMEM),
             pl.BlockSpec((per_step * HEAD, HEAD), lambda h: (h, 0)),
             pl.BlockSpec((1, per_step * HEAD), lambda h: (0, h)),
         ],
         out_specs=block,
         out_shape=jax.ShapeDtypeStruct((length, width), BF16),
         scratch_shapes=[pltpu.VMEM((length, HEAD), BF16)],
-        compiler_params=pltpu.CompilerParams(vmem_limit_bytes=56 * 1024 * 1024),
+        compiler_params=pltpu.CompilerParams(vmem_limit_bytes=12 * 1024 * 1024),
         name="finish",
     )(tile_doc, tile_fill, prev, queries, raw, carry, gain.reshape(1, width))
 
 
 def solution(mesh):
     def body(queries, keys, values, gain, tile_doc, tile_fill):
-        raw, carry, prev = local_part(mesh, queries, keys, values, tile_doc, tile_fill)
-        return finish(queries, raw, gain, tile_doc, tile_fill, carry, prev)
+        raw, held, carry, prev = local_part(mesh, queries, keys, values, tile_doc, tile_fill)
+        return finish(held, raw, gain, tile_doc, tile_fill, carry, prev)
 
     rows = P(("outer", "inner"), None)
     tiles = P(("outer", "inner"))

time: 58.6 us -> 52.3 us (0.89)
  Pallas kernels: 58.4 us -> 50.8 us
  local copies, waits for them, and re-layouts: 0 us -> 1.31 us
    pallas_call x1, Pallas kernels: 14.3 us -> 8.11 us  [finish(): pl.pallas_call(functools.partial(finish_kernel, length // TILE, per_step)...]
    pallas_call x1, Pallas kernels: 44.2 us -> 42.7 us  [local_part(): pl.pallas_call(functools.partial(local_kernel, outer, inner, length // TI...]
    unnamed x0 -> x6, local copies, waits for them, and re-layouts: none -> 1.31 us
where the time goes in v3:
time: 52.3 us; the launch traced here: 52.2 us
  Pallas kernels  50.8 us (97%)
  local copies, waits for them, and re-layouts  1.31 us (3%)
    pallas_call x1, Pallas kernels, local_part(): pl.pallas_call(functools.partial(local_kernel, outer, inner, length // TI...  42.7 us
    pallas_call x1, Pallas kernels, finish(): pl.pallas_call(functools.partial(finish_kernel, length // TILE, per_step)...  8.11 us
    unnamed x6, local copies, waits for them, and re-layouts  1.31 us

profile of v3, /device:TPU:0, one launch (start us, length us, event | category | flops | bytes accessed | tf_op | source)
XLA Modules:
  0.0 52.2 jit_solution(10039371177916080873)
XLA Ops:
  0.0 0.0 copy-start.1
  0.0 0.7 %copy-done.1 = s32[12]{0:T(128)S(1)} copy-done((s32[12]{0:T(128)S(1)}, s32[12]{0:T(128)}, u32[]{:S(2)}) %copy-start.1) | copy-done | bytes 72
  0.7 0.0 copy-start.2
  0.7 0.7 %copy-done.2 = s32[12]{0:T(128)S(1)} copy-done((s32[12]{0:T(128)S(1)}, s32[12]{0:T(128)}, u32[]{:S(2)}) %copy-start.2) | copy-done | bytes 72
  1.3 0.0 copy-start
  1.3 42.7 %local_part.1 = (f32[1536,2048]{1,0:T(8,128)S(1)}, bf16[1536,2048]{1,0:T(8,128)(2,1)S(1)}, f32[2048,128]{1,0:T(8,128)S(1)}, f32[8,128]{1,0:T(8,128)S(1)}) custom-call(s32[12]{0:T(128)S(1)} %copy-done.1, s32[12]{0:T(128)S(1)} %copy-done.2, bf16[1536,2048]{1,0:T(8,128)(2,1)} %query_hbm.1, bf16[1536,2048]{1,0:T(8,128)(2,1)} %key_hbm.1, bf16[1536,2048]{1,0:T(8,128)(2,1)} %value_hbm.1), custom_call_target="tpu_custom_call" | custom-call | tf_op jit(solution)/shard_map/local_part/pallas_call | solution.py:290
  44.1 0.0 copy-done
  44.1 8.1 %finish.1 = bf16[1536,2048]{1,0:T(8,128)(2,1)} custom-call(s32[12]{0:T(128)S(1)} %copy-done.1, s32[12]{0:T(128)S(1)} %copy-done.2, f32[8,128]{1,0:T(8,128)S(1)} %get-tuple-element.9.prev_ref, bf16[1536,2048]{1,0:T(8,128)(2,1)S(1)} %get-tuple-element.10.query_ref, f32[1536,2048]{1,0:T(8,128)S(1)} %get-tuple-element.11.raw_ref, ...), custom_call_target="tpu_custom_call" | custom-call | tf_op jit(solution)/shard_map/finish/pallas_call | solution.py:347
Async XLA Ops:
  0.0 0.7 %copy-start.1 = (s32[12]{0:T(128)S(1)}, s32[12]{0:T(128)}, u32[]{:S(2)}) copy-start(s32[12]{0:T(128)} %doc_ref.3) | copy-start | bytes 148
  0.7 0.7 %copy-start.2 = (s32[12]{0:T(128)S(1)}, s32[12]{0:T(128)}, u32[]{:S(2)}) copy-start(s32[12]{0:T(128)} %fill_ref.3) | copy-start | bytes 148
  1.3 42.7 %copy-start = (f32[2048]{0:T(1024)S(1)}, f32[2048]{0:T(1024)}, u32[]{:S(2)}) copy-start(f32[2048]{0:T(1024)} %param.9) | copy-start | bytes 24580

commit v4 on v3

--- a/solution.py
+++ b/solution.py
@@ -61,7 +61,7 @@
 
 def local_kernel(
     outer, inner, tiles, heads, chunks,
-    doc_ref, fill_ref, query_hbm, key_hbm, value_hbm, raw_ref, query_ref, carry_ref, prev_ref,
+    doc_ref, fill_ref, query_hbm, key_hbm, value_hbm, raw_ref, query_ref, carry_ref, enters_ref,
     key_ref, value_ref, state_ref,
     real_ref, last_ref, uses_ref, pair_ref,
     swap_out, swap_in, out1, in1, out3, in3, back_out, back_in,
@@ -223,7 +223,8 @@
     in1[0] = out1[0]
     for c in range(chunks):
         load(2, c).wait()
-    run(0, heads // 2, local)
+    early = (heads - 2) // 2
+    run(0, early, local)
     run(1, chips, lambda k: copy1(k).wait())
 
     def lap(c, so_far):
@@ -242,12 +243,12 @@
 
     run(1, chips, lambda k: copy3(k).start())
     in3[0] = out3[0]
-    run(heads // 2, heads, local)
+    run(early, heads - 2, local)
     run(1, chips, lambda k: copy3(k).wait())
 
     before = in3[0, pl.ds(part, 8), :]
     keep0 = (doc0 == before).astype(F32)[0:1, :]
-    prev_ref[...] = jnp.where(first_core, before, doc0)
+    entered = jnp.where(first_core, before, doc0)[0:1, :]
 
     def unpack(k, _):
         source = (chip - k + chips) % chips
@@ -265,6 +266,12 @@
         back_out, back_in, back_sems.at[0], back_sems.at[1], device_id=twin, device_id_type=MESH
     )
     back.start()
+    for tile in range(tiles):
+        rows = pl.ds(tile * TILE, TILE)
+        doc = jnp.full((1, HEAD), doc_ref[tile], jnp.int32).astype(F32)
+        same = (doc == entered).astype(F32)
+        enters_ref[rows, :] = (real_ref[rows, :].astype(F32) * same).astype(BF16)
+    run(heads - 2, heads, local)
     back.wait()
     carry_ref[pl.ds((1 - core) * half, half), :] = back_in[...]
 
@@ -295,7 +302,7 @@
             pltpu.VMEM((length, width), F32),
             pltpu.VMEM((length, width), BF16),
             jax.ShapeDtypeStruct((width, HEAD), F32),
-            jax.ShapeDtypeStruct((8, HEAD), F32),
+            jax.ShapeDtypeStruct((length, HEAD), BF16),
         ],
         scratch_shapes=[
             rows, rows,
@@ -313,24 +320,12 @@
     )(tile_doc, tile_fill, queries, keys, values)
 
 
-def finish_kernel(
-    tiles, per_step,
-    doc_ref, fill_ref, prev_ref, query_ref, raw_ref, carry_ref, gain_ref, out_ref, uses_ref,
-):
-    @pl.when(pl.program_id(0) == 0)
-    def _():
-        entering = prev_ref[0:1, :]
-        for tile in range(tiles):
-            doc = jnp.full((1, HEAD), doc_ref[tile], jnp.int32).astype(F32)
-            same = (doc == entering).astype(F32)
-            real = rows_below(fill_ref[tile]).astype(F32)
-            uses_ref[pl.ds(tile * TILE, TILE), :] = (real * same).astype(BF16)
-
+def finish_kernel(per_step, enters_ref, query_ref, raw_ref, carry_ref, gain_ref, out_ref):
     for head in range(per_step):
         cols = slice(head * HEAD, (head + 1) * HEAD)
         begin = (pl.program_id(0) * per_step + head) * HEAD
         here = pl.ds(pl.multiple_of(begin, HEAD), HEAD)
-        using = query_ref[:, here] * uses_ref[...]
+        using = query_ref[:, here] * enters_ref[...]
         twice = jnp.concatenate([using, using], axis=1)
         raw = raw_ref[:, here]
         raw = raw + dot(twice, split(carry_ref[cols, :]), ((1,), (0,)))
@@ -338,36 +333,32 @@
         out_ref[:, cols] = (raw * lax.rsqrt(meansq + 1e-06) * gain_ref[:, cols]).astype(BF16)
 
 
-def finish(queries, raw, gain, tile_doc, tile_fill, carry, prev):
+def finish(queries, raw, gain, carry, enters):
     length, width = queries.shape
     heads = width // HEAD
     per_step = 2
-    block = pl.BlockSpec((length, per_step * HEAD), lambda h: (0, h))
-    smem = pl.BlockSpec(memory_space=pltpu.SMEM)
+    vmem = pl.BlockSpec(memory_space=pltpu.VMEM)
     return pl.pallas_call(
-        functools.partial(finish_kernel, length // TILE, per_step),
+        functools.partial(finish_kernel, per_step),
         grid=(heads // per_step,),
         in_specs=[
-            smem,
-            smem,
-            pl.BlockSpec((8, HEAD), lambda h: (0, 0)),
-            pl.BlockSpec(memory_space=pltpu.VMEM),
-            pl.BlockSpec(memory_space=pltpu.VMEM),
+            vmem,
+            vmem,
+            vmem,
             pl.BlockSpec((per_step * HEAD, HEAD), lambda h: (h, 0)),
             pl.BlockSpec((1, per_step * HEAD), lambda h: (0, h)),
         ],
-        out_specs=block,
+        out_specs=pl.BlockSpec((length, per_step * HEAD), lambda h: (0, h)),
         out_shape=jax.ShapeDtypeStruct((length, width), BF16),
-        scratch_shapes=[pltpu.VMEM((length, HEAD), BF16)],
         compiler_params=pltpu.CompilerParams(vmem_limit_bytes=12 * 1024 * 1024),
         name="finish",
-    )(tile_doc, tile_fill, prev, queries, raw, carry, gain.reshape(1, width))
+    )(enters, queries, raw, carry, gain.reshape(1, width))
 
 
 def solution(mesh):
     def body(queries, keys, values, gain, tile_doc, tile_fill):
-        raw, held, carry, prev = local_part(mesh, queries, keys, values, tile_doc, tile_fill)
-        return finish(held, raw, gain, tile_doc, tile_fill, carry, prev)
+        raw, held, carry, enters = local_part(mesh, queries, keys, values, tile_doc, tile_fill)
+        return finish(held, raw, gain, carry, enters)
 
     rows = P(("outer", "inner"), None)
     tiles = P(("outer", "inner"))

time: 52.3 us -> 53.1 us (1.015)
  Pallas kernels: 50.8 us -> 51.6 us
    pallas_call x1, Pallas kernels: 42.7 us -> 44.2 us  [local_part(): pl.pallas_call(functools.partial(local_kernel, outer, inner, length // TI...]
    pallas_call x1, Pallas kernels: 8.11 us -> 7.41 us  [finish(): pl.pallas_call(functools.partial(finish_kernel, per_step), grid=(heads //...]
where the time goes in v4:
time: 53.1 us; the launch traced here: 52.9 us
  Pallas kernels  51.6 us (97%)
  local copies, waits for them, and re-layouts  1.31 us (2%)
    pallas_call x1, Pallas kernels, local_part(): pl.pallas_call(functools.partial(local_kernel, outer, inner, length // TI...  44.2 us
    pallas_call x1, Pallas kernels, finish(): pl.pallas_call(functools.partial(finish_kernel, per_step), grid=(heads //...  7.41 us
    unnamed x6, local copies, waits for them, and re-layouts  1.31 us

profile of v4, /device:TPU:0, one launch (start us, length us, event | category | flops | bytes accessed | tf_op | source)
XLA Modules:
  0.0 52.9 jit_solution(687636950933313711)
XLA Ops:
  0.0 0.0 copy-start.1
  0.0 0.7 %copy-done.1 = s32[12]{0:T(128)S(1)} copy-done((s32[12]{0:T(128)S(1)}, s32[12]{0:T(128)}, u32[]{:S(2)}) %copy-start.1) | copy-done | bytes 72
  0.7 0.0 copy-start.2
  0.7 0.7 %copy-done.2 = s32[12]{0:T(128)S(1)} copy-done((s32[12]{0:T(128)S(1)}, s32[12]{0:T(128)}, u32[]{:S(2)}) %copy-start.2) | copy-done | bytes 72
  1.3 0.0 copy-start
  1.3 44.2 %local_part.1 = (f32[1536,2048]{1,0:T(8,128)S(1)}, bf16[1536,2048]{1,0:T(8,128)(2,1)S(1)}, f32[2048,128]{1,0:T(8,128)S(1)}, bf16[1536,128]{1,0:T(8,128)(2,1)S(1)}) custom-call(s32[12]{0:T(128)S(1)} %copy-done.1, s32[12]{0:T(128)S(1)} %copy-done.2, bf16[1536,2048]{1,0:T(8,128)(2,1)} %query_hbm.1, bf16[1536,2048]{1,0:T(8,128)(2,1)} %key_hbm.1, ...), custom_call_target="tpu_custom_call" | custom-call | tf_op jit(solution)/shard_map/local_part/pallas_call | solution.py:297
  45.5 0.0 copy-done
  45.5 7.4 %finish.1 = bf16[1536,2048]{1,0:T(8,128)(2,1)} custom-call(bf16[1536,128]{1,0:T(8,128)(2,1)S(1)} %get-tuple-element.9.enters_ref, bf16[1536,2048]{1,0:T(8,128)(2,1)S(1)} %get-tuple-element.10.query_ref, f32[1536,2048]{1,0:T(8,128)S(1)} %get-tuple-element.11.raw_ref, f32[2048,128]{1,0:T(8,128)S(1)} %get-tuple-element.12.carry_ref, f32[1,2048]{1,0:T(1,128)S(1)} %bitcast.1), custom_call_target="tpu_custom_call" | custom-call | tf_op jit(solution)/shard_map/finish/pallas_call | solution.py:341
Async XLA Ops:
  0.0 0.7 %copy-start.1 = (s32[12]{0:T(128)S(1)}, s32[12]{0:T(128)}, u32[]{:S(2)}) copy-start(s32[12]{0:T(128)} %doc_ref.1) | copy-start | bytes 148
  0.7 0.7 %copy-start.2 = (s32[12]{0:T(128)S(1)}, s32[12]{0:T(128)}, u32[]{:S(2)}) copy-start(s32[12]{0:T(128)} %fill_ref.1) | copy-start | bytes 148
  1.3 44.2 %copy-start = (f32[2048]{0:T(1024)S(1)}, f32[2048]{0:T(1024)}, u32[]{:S(2)}) copy-start(f32[2048]{0:T(1024)} %param.9) | copy-start | bytes 24580
